TPU v7x, 32 devices: a whole 2x2x4 slice. The times are simulated.
32 devices in a mesh: chan: 4 (over y, x), tm: 8 (over z, core).
Axes of the slice: x: 2, y: 2, z: 4, core: 2. Of those that a mesh axis runs over, the one named last changes fastest.
Arguments:
- traces: bfloat16 [64, 512, 2048], P('tm', 'chan'), may hold values from -6 to 6
- live: int32 [512], P('chan'), may hold values 0 or 1
Outputs:
- correlations: bfloat16 [512, 128, 2048], P(('chan', 'tm'))
Inputs may be any that keep to these rules, and one draw needn't show every extreme that they name: `live`: 1 marks a usable channel, 0 a dead one.
All inputs are finite; a program needn't handle non-finite values. No bound on the sum of `live` on one device may be relied on, other than what follows from the above.
Results may differ from a plain program's by a relative error of at most 0.0076.
Values may be sent and summed in bfloat16 or wider, within the bound.
A program may use at most 128 MiB of HBM per device.

v0:
```python
import math

import jax
import jax.numpy as jnp
from jax import lax
from jax.sharding import PartitionSpec as P

SMOOTH = 4


def from_behind(block, axis, distance):
    devices = range(lax.axis_size(axis))
    route = [(i - distance, i) for i in devices if i - distance in devices]
    return lax.ppermute(block, axis, route)


def column_bins(count, group_width):
    index = jnp.arange(count, dtype=jnp.int32)
    group = index // (2 * group_width)
    within = index % group_width
    is_imag = index // group_width % 2
    return (group * group_width + within, is_imag)


def forward_table(samples, bins, group_width):
    freq, is_imag = column_bins(2 * bins, group_width)
    moments = jnp.arange(samples, dtype=jnp.int32)[:, None]
    phase = (moments * freq[None, :] % samples).astype(jnp.float32) * (2.0 * math.pi / samples)
    return jnp.where(is_imag[None, :] == 1, -jnp.sin(phase), jnp.cos(phase)).astype(jnp.bfloat16)


def inverse_table(samples, bins, group_width, segments):
    freq, is_imag = column_bins(2 * bins, group_width)
    lag = jnp.arange(samples, dtype=jnp.int32) - samples // 2
    phase = jnp.mod(freq[:, None] * lag[None, :], samples).astype(jnp.float32) * (
        2.0 * math.pi / samples
    )
    weight = jnp.where(freq == 0, 1.0, 2.0).astype(jnp.float32) / math.sqrt(samples * segments)
    wave = jnp.where(is_imag[:, None] == 1, -jnp.sin(phase), jnp.cos(phase))
    return (weight[:, None] * wave).astype(jnp.bfloat16)


def whiten(spectra, groups):
    lead = spectra.shape[:-1]
    bins = spectra.shape[-1] // 2
    width = bins // groups
    split = spectra.reshape(lead + (groups, 2, width))
    real_part = split[..., 0, :].reshape(lead + (bins,))
    imag_part = split[..., 1, :].reshape(lead + (bins,))
    amplitude = jnp.sqrt(real_part * real_part + imag_part * imag_part)
    padded = jnp.pad(amplitude, [(0, 0)] * len(lead) + [(SMOOTH, SMOOTH)])
    smooth = sum((padded[..., i : i + bins] for i in range(2 * SMOOTH + 1))) / (2 * SMOOTH + 1)
    water = 0.8 * jnp.mean(amplitude, axis=-1, keepdims=True) + 1e-06
    level = jnp.maximum(smooth, water).reshape(lead + (groups, 1, width))
    return (split / level).reshape(lead + (2 * bins,)).astype(jnp.bfloat16)


def band(matrix):
    rows, width, extra = matrix.shape
    flat = matrix.reshape(rows * width, extra)
    flat = jnp.pad(flat, ((0, rows), (0, 0)))
    return flat.reshape(rows, width + 1, extra)[:, 1 : rows + 1, :]


def product(left, right):
    return jnp.einsum("sah,sbh->abh", left, right, preferred_element_type=jnp.float32)


def cross(own_white, extended, own_flags, ext_flags, half):
    own_real = own_white[..., :half]
    own_imag = own_white[..., half:]
    ext_real = extended[..., :half]
    ext_imag = extended[..., half:]
    real_sum = product(own_real, ext_real) + product(own_imag, ext_imag)
    imag_sum = product(own_imag, ext_real) - product(own_real, ext_imag)
    pair_flags = band((own_flags[:, None] * ext_flags[None, :])[:, :, None])
    both = jnp.concatenate([band(real_sum), band(imag_sum)], axis=-1)
    return (both * pair_flags).astype(jnp.bfloat16)


def transform_rows(traces_part, table, groups):
    seg_dev, rows, samples = traces_part.shape
    spectra = jnp.dot(
        traces_part.reshape(seg_dev * rows, samples), table, preferred_element_type=jnp.float32
    )
    return whiten(spectra.reshape(seg_dev, rows, table.shape[1]), groups)


def body(traces, live):
    seg_dev, block, samples = traces.shape
    bins = samples // 2
    groups = lax.axis_size("tm")
    group_width = bins // groups
    segments = seg_dev * groups
    table = forward_table(samples, bins, group_width)
    inverse = inverse_table(samples, bins, group_width, segments)
    flags = live.astype(jnp.bfloat16)
    white = transform_rows(traces, table, groups)
    own_white = lax.all_to_all(white, "tm", split_axis=2, concat_axis=0, tiled=True)
    next_white, next_flags = from_behind((own_white, flags), "chan", -1)
    extended = jnp.concatenate([own_white, next_white], axis=1)
    ext_flags = jnp.concatenate([flags, next_flags], axis=0).astype(jnp.float32)
    stack = cross(own_white, extended, flags.astype(jnp.float32), ext_flags, group_width)
    lagged = jnp.einsum(
        "rif,fl->ril",
        lax.all_to_all(stack, "tm", split_axis=0, concat_axis=2, tiled=True),
        inverse,
        preferred_element_type=jnp.float32,
    )
    return lagged.astype(jnp.bfloat16)


def solution(mesh):
    in_specs = (P("tm", "chan", None), P("chan"))
    out_specs = P(("chan", "tm"), None, None)
    return jax.shard_map(body, mesh=mesh, in_specs=in_specs, out_specs=out_specs, check_vma=False)
```

profile of v0, /device:TPU:13, one launch (start us, length us, event | category | flops | bytes accessed | tf_op | source)
XLA Modules:
  0.0 765.0 jit_solution(12830453108012143887)
XLA Ops:
  0.6 67.4 %select_convert_fusion.4 = bf16[2048,2048]{1,0:T(8,128)(2,1)S(1)} fusion(s32[2048]{0:T(1024)S(1)} %fusion.60, pred[2048]{0:T(1024)(128)(4,1)S(1)} %fusion.57), kind=kLoop, calls=%fused_computation.19.clone.clone.1 | loop fusion | flops 71303168 | bytes 8398848 | tf_op jit(solution)/shard_map/dot_general | solution.py:83
  68.0 11.0 %fusion.13 = f32[2048,1024]{0,1:T(8,128)} fusion(bf16[1024,2048]{1,0:T(8,128)(2,1)S(1)} %bitcast.56, bf16[2048,2048]{1,0:T(8,128)(2,1)S(1)} %select_convert_fusion.4), kind=kOutput, calls=%fused_computation.25 | convolution fusion | flops 8589934592 | bytes 20971520 | tf_op jit(solution)/shard_map/dot_general | solution.py:83
  79.0 11.7 %reshape_reshape.6 = f32[8,128,8,2,128]{4,3,2,1,0:T(2,128)} reshape(f32[1024,2048]{1,0:T(8,128)} %bitcast.50) | data formatting | bytes 16777216 | tf_op jit(solution)/shard_map/reshape;reshape | solution.py:47
  91.3 37.4 %fusion.71 = (f32[8,128]{1,0:T(8,128)S(1)}, f32[8,128,8,128]{3,2,1,0:T(8,128)}) fusion(f32[]{:T(128)} %broadcast.340, f32[8,128,8,2,128]{4,3,2,1,0:T(2,128)} %reshape_reshape.6), kind=kLoop, calls=%fused_computation.112 | loop fusion | flops 4193280 | bytes 12587012 | tf_op jit(solution)/shard_map/reduce_sum | solution.py:53
  133.6 23.6 %fusion.41 = f32[8,128,1024]{2,1,0:T(8,128)} fusion(f32[8,128,1024]{2,1,0:T(8,128)} %sqrt.8, f32[8,128]{1,0:T(8,128)S(1)} %multiply_add_fusion), kind=kLoop, calls=%fused_computation.61 | loop fusion | flops 10485760 | bytes 8392704 | tf_op jit(solution)/shard_map/max | solution.py:54
  162.6 9.3 %copy.9 = f32[8,128,2048]{1,0,2:T(8,128)} copy(f32[8,128,2048]{2,1,0:T(8,128)} %bitcast.51) | data formatting | bytes 16777216 | tf_op jit(solution)/shard_map/reshape;reshape | solution.py:47
  177.0 96.3 %all_to_all.36 = bf16[8,128,2048]{1,0,2:T(8,128)(2,1)S(1)} all-to-all(bf16[8,128,2048]{1,0,2:T(8,128)(2,1)S(1)} %fusion.14), channel_id=1, replica_groups=mesh['chan'=4,'tm'=8] {'tm'}, dimensions={2} | all-to-all | bytes 8388608 | tf_op jit(solution)/shard_map/all_to_all | solution.py:99
  282.0 87.7 %collective-permute-done.1 = bf16[128]{0:T(256)(128)(2,1)S(1)} collective-permute-done((bf16[128]{0:T(256)(128)(2,1)S(1)}, bf16[128]{0:T(256)(128)(2,1)S(1)}, u32[]{:S(2)}, u32[]{:S(2)}) %collective-permute-start.1) | collective-permute-done | bytes 288 | tf_op jit(solution)/shard_map/ppermute | solution.py:14
  371.3 10.9 %fusion.45 = f32[128,256,128]{2,1,0:T(8,128)} fusion(bf16[64,128,256]{1,0,2:T(8,128)(2,1)} %bitcast.47, bf16[64,128,256]{1,0,2:T(8,128)(2,1)} %collective-permute-done), kind=kOutput, calls=%fused_computation.68 | convolution fusion | flops 553648128 | bytes 27262976 | tf_op jit(solution)/shard_map/sah,sbh->abh/dot_general | solution.py:66
  382.3 16.1 %add_bitcast_fusion = f32[128,256,128]{0,1,2:T(8,128)} fusion(f32[128,256,128]{2,1,0:T(8,128)} %fusion.45, bf16[64,128,256]{1,0,2:T(8,128)(2,1)} %bitcast.47, bf16[64,128,256]{1,0,2:T(8,128)(2,1)} %collective-permute-done), kind=kOutput, calls=%fused_computation.18 | convolution fusion | flops 557842432 | bytes 44040192 | tf_op jit(solution)/shard_map/sah,sbh->abh/dot_general | solution.py:66
  398.3 17.9 %copy.11 = f32[128,256,128]{2,1,0:T(8,128)} copy(f32[128,256,128]{0,1,2:T(8,128)} %add_bitcast_fusion) | data formatting | bytes 33554432 | tf_op jit(solution)/shard_map/add | solution.py:74
  416.2 13.3 %pad.16 = f32[32896,128]{1,0:T(8,128)} pad(f32[32768,128]{1,0:T(8,128)} %bitcast.49, f32[]{:T(128)} %constant.116.clone.1), padding=0_128x0_0 | pad | bytes 33619972 | tf_op jit(solution)/shard_map/jit(_pad)/pad | solution.py:61
  429.5 17.5 %reshape.174 = f32[128,257,128]{2,1,0:T(8,128)} reshape(f32[32896,128]{1,0:T(8,128)} %pad.16) | data formatting | bytes 33685504 | tf_op jit(solution)/shard_map/reshape | solution.py:62
  447.0 8.3 %slice.73 = f32[128,128,128]{2,1,0:T(8,128)} slice(f32[128,257,128]{2,1,0:T(8,128)} %reshape.174), slice={[0:128], [1:129], [0:128]} | slice | bytes 16777216 | tf_op jit(solution)/shard_map/slice | solution.py:62
  455.2 10.9 %fusion.47 = f32[128,256,128]{2,1,0:T(8,128)} fusion(bf16[64,128,256]{1,0,2:T(8,128)(2,1)} %bitcast.47, bf16[64,128,256]{1,0,2:T(8,128)(2,1)} %collective-permute-done), kind=kOutput, calls=%fused_computation.70 | convolution fusion | flops 553648128 | bytes 27262976 | tf_op jit(solution)/shard_map/sah,sbh->abh/dot_general | solution.py:66
  466.2 16.1 %subtract_bitcast_fusion = f32[128,256,128]{0,1,2:T(8,128)} fusion(f32[128,256,128]{2,1,0:T(8,128)} %fusion.47, bf16[64,128,256]{1,0,2:T(8,128)(2,1)} %bitcast.47, bf16[64,128,256]{1,0,2:T(8,128)(2,1)} %collective-permute-done), kind=kOutput, calls=%fused_computation.17 | convolution fusion | flops 557842432 | bytes 44040192 | tf_op jit(solution)/shard_map/sah,sbh->abh/dot_general | solution.py:66
  482.2 17.6 %copy.12 = f32[128,256,128]{2,1,0:T(8,128)} copy(f32[128,256,128]{0,1,2:T(8,128)} %subtract_bitcast_fusion) | data formatting | bytes 33554432 | tf_op jit(solution)/shard_map/sub | solution.py:75
  499.9 13.3 %pad.17 = f32[32896,128]{1,0:T(8,128)} pad(f32[32768,128]{1,0:T(8,128)} %bitcast.48, f32[]{:T(128)} %constant.116.clone.1), padding=0_128x0_0 | pad | bytes 33619972 | tf_op jit(solution)/shard_map/jit(_pad)/pad | solution.py:61
  513.2 17.5 %reshape.176 = f32[128,257,128]{2,1,0:T(8,128)} reshape(f32[32896,128]{1,0:T(8,128)} %pad.17) | data formatting | bytes 33685504 | tf_op jit(solution)/shard_map/reshape | solution.py:62
  535.5 7.9 %fusion.6 = bf16[128,128,256]{2,1,0:T(8,128)(2,1)} fusion(f32[128,128,128]{2,1,0:T(8,128)S(1)} %slice.74, f32[128,128,128]{2,1,0:T(8,128)} %slice.73, f32[128,128]{1,0:T(8,128)S(1)} %copy-done), kind=kLoop, calls=%fused_computation.15 | loop fusion | flops 12582912 | bytes 25231360 | tf_op jit(solution)/shard_map/convert_element_type | solution.py:78
  543.5 9.4 %all-to-all-start.1 = ((bf16[128,128,256]{2,1,0:T(8,128)(2,1)}), bf16[128,128,256]{2,1,0:T(8,128)(2,1)}, u32[]{:S(2)}, u32[]{:S(2)}) async-start(bf16[128,128,256]{2,1,0:T(8,128)(2,1)} %fusion.6), calls=%async_computation.1 | async-start | bytes 16777216 | tf_op jit(solution)/shard_map/all_to_all | solution.py:106
  552.9 71.1 %fusion.79 = bf16[2048,2048,1]{1,0,2:T(8,128)(2,1)} fusion(s32[2048]{0:T(1024)S(1)} %iota_add_fusion, s32[2048]{0:T(1024)S(1)} %copy-done.2, f32[2048]{0:T(1024)S(1)} %select_multiply_fusion, pred[2048]{0:T(1024)(128)(4,1)S(1)} %copy-done.4), kind=kLoop, calls=%fused_computation.23.clone.clone.clone.clone.1 | loop fusion | flops 75497472 | bytes 8415232 | tf_op jit(solution)/shard_map/rif,fl->ril/dot_general | solution.py:104
  624.1 109.1 %all-to-all-done.1 = bf16[128,128,256]{2,1,0:T(8,128)(2,1)} async-done(((bf16[128,128,256]{2,1,0:T(8,128)(2,1)}), bf16[128,128,256]{2,1,0:T(8,128)(2,1)}, u32[]{:S(2)}, u32[]{:S(2)}) %all-to-all-start.1) | async-done | bytes 8388640 | tf_op jit(solution)/shard_map/all_to_all | solution.py:106
  741.0 23.5 %fusion.29 = bf16[16,128,2048]{2,1,0:T(8,128)(2,1)} fusion(bf16[16,128,2048]{2,1,0:T(8,128)(2,1)} %bitcast.54, bf16[2048,2048,1]{1,0,2:T(8,128)(2,1)} %fusion.79), kind=kOutput, calls=%fused_computation.43 | convolution fusion | flops 17184063488 | bytes 25165824 | tf_op jit(solution)/shard_map/rif,fl->ril/dot_general | solution.py:104
  (36 shorter events, 39.4 us)
Async XLA Ops:
  0.0 68.0 %copy-start.5 = (bf16[8,128,2048]{2,1,0:T(8,128)(2,1)S(1)}, bf16[8,128,2048]{2,1,0:T(8,128)(2,1)}, u32[]{:S(2)}) copy-start(bf16[8,128,2048]{2,1,0:T(8,128)(2,1)} %param.2) | copy-start | bytes 12582916
  0.0 0.6 copy-start.1
  0.6 67.4 %copy-start.3 = (pred[2048]{0:T(1024)(128)(4,1)}, pred[2048]{0:T(1024)(128)(4,1)S(1)}, u32[]{:S(2)}) copy-start(pred[2048]{0:T(1024)(128)(4,1)S(1)} %fusion.57) | copy-start | bytes 6148
  176.9 102.7 %copy-start.6 = (s32[128]{0:T(128)S(1)}, s32[128]{0:T(128)}, u32[]{:S(2)}) copy-start(s32[128]{0:T(128)} %param.3) | copy-start | bytes 1540
  276.6 94.8 %collective-permute-start = (bf16[64,128,256]{1,0,2:T(8,128)(2,1)}, bf16[64,128,256]{1,0,2:T(8,128)(2,1)}, u32[]{:S(2)}, u32[]{:S(2)}) collective-permute-start(bf16[64,128,256]{1,0,2:T(8,128)(2,1)} %bitcast.47), channel_id=1, source_target_pairs={{8,0},{16,8},{24,16},{9,1},{17,9},{25,17},{10,2},{18,10},{26,18},{... | collective-permute-start | bytes 12582920 | tf_op jit(solution)/shard_map/ppermute | solution.py:14
  279.6 90.1 %collective-permute-start.1 = (bf16[128]{0:T(256)(128)(2,1)S(1)}, bf16[128]{0:T(256)(128)(2,1)S(1)}, u32[]{:S(2)}, u32[]{:S(2)}) collective-permute-start(bf16[128]{0:T(256)(128)(2,1)S(1)} %get-tuple-element.8), channel_id=1, source_target_pairs={{8,0},{16,8},{24,16},{9,1},{17,9},{25,17},{10,2},{18,10},{26,18},{... | collective-permute-start | bytes 776 | tf_op jit(solution)/shard_map/ppermute | solution.py:14
  530.6 4.9 copy-start
  543.5 9.4 %copy-start.2 = (s32[2048]{0:T(1024)S(1)}, s32[2048]{0:T(1024)}, u32[]{:S(2)}) copy-start(s32[2048]{0:T(1024)} %copy-done.1) | copy-start | bytes 24580
  543.5 9.5 %copy-start.4 = (pred[2048]{0:T(1024)(128)(4,1)S(1)}, pred[2048]{0:T(1024)(128)(4,1)}, u32[]{:S(2)}) copy-start(pred[2048]{0:T(1024)(128)(4,1)} %copy-done.3) | copy-start | bytes 6148
  543.5 189.7 %all-to-all-start.1 = ((bf16[128,128,256]{2,1,0:T(8,128)(2,1)}), bf16[128,128,256]{2,1,0:T(8,128)(2,1)}, u32[]{:S(2)}, u32[]{:S(2)}) async-start(bf16[128,128,256]{2,1,0:T(8,128)(2,1)} %fusion.6), calls=%async_computation.1 | async-start | bytes 16777216 | tf_op jit(solution)/shard_map/all_to_all | solution.py:106
where the time goes:
time: 778 us; the launch traced here: 765 us
  other arithmetic  213 us (27%)
  waiting for transfers between devices  197 us (25%)
  local copies, waits for them, and re-layouts  155 us (20%)
  blocking collectives  96.3 us (12%)
  matrix products  88.6 us (11%)
  starting transfers between devices  14.8 us (2%)
    all_to_all x1, waiting for transfers between devices, body(): lax.all_to_all(stack, 'tm', split_axis=0, concat_axis=2, tiled=True)  109 us
    all_to_all x1, blocking collectives, body(): lax.all_to_all(white, 'tm', split_axis=2, concat_axis=0, tiled=True)  96.3 us
    ppermute x2, waiting for transfers between devices, from_behind(): return lax.ppermute(block, axis, route)  87.7 us
    dot_general x1, other arithmetic, body(): jnp.einsum('rif,fl->ril', lax.all_to_all(stack, 'tm', split_axis=0, conca...  71.1 us
    dot_general x1, other arithmetic, transform_rows(): jnp.dot(traces_part.reshape(seg_dev * rows, samples), table, preferred_el...  67.4 us
    dot_general x4, matrix products, product(): jnp.einsum('sah,sbh->abh', left, right, preferred_element_type=jnp.float32)  54 us
    reduce_sum x1, other arithmetic, whiten(): water = 0.8 * jnp.mean(amplitude, axis=-1, keepdims=True) + 1e-06  37.4 us
    reshape x3, local copies, waits for them, and re-layouts, band(): return flat.reshape(rows, width + 1, extra)[:, 1:rows + 1, :]  35.3 us
  transfers between devices with their start and end apart: 3, of which 2 were waited for; matrix products, arithmetic and copies ran while one was open for 10% of the time, Pallas kernels for 0%

commit v1 on v0

v1 whole, which is shorter than its diff:
```python
import functools
import math

import jax
import jax.numpy as jnp
import ml_dtypes
import numpy as np
from jax import lax
from jax.experimental import pallas as pl
from jax.experimental.pallas import tpu as pltpu
from jax.sharding import PartitionSpec as P

SMOOTH = 4
MIB = 1 << 20


def from_behind(block, axis, distance):
    devices = range(lax.axis_size(axis))
    route = [(i - distance, i) for i in devices if i - distance in devices]
    return lax.ppermute(block, axis, route)


def forward_rows(samples, bins):
    phase = np.outer(np.arange(bins), np.arange(samples)) % samples
    angle = phase * (2.0 * math.pi / samples)
    return np.concatenate([np.cos(angle), -np.sin(angle)], axis=0).astype(ml_dtypes.bfloat16)


def inverse_rows(samples, bins, groups, segments):
    lag = np.arange(samples) - samples // 2
    phase = np.mod(np.outer(np.arange(bins), lag), samples)
    angle = phase * (2.0 * math.pi / samples)
    weight = np.where(np.arange(bins) == 0, 1.0, 2.0)[:, None] / math.sqrt(samples * segments)
    width = bins // groups
    wave = np.stack([weight * np.cos(angle), -weight * np.sin(angle)])
    wave = wave.reshape(2, groups, width, samples).transpose(1, 0, 2, 3)
    return wave.reshape(2 * bins, samples).astype(ml_dtypes.bfloat16)


def whiten_kernel(pair, traces_ref, table_ref, white_ref, padded, held):
    _, block, samples = traces_ref.shape
    bins = samples // 2
    segs = held.shape[0] // bins // 2
    step = pl.program_id(0)
    rows = traces_ref[...].reshape(pair * block, samples)
    spectra = lax.dot_general(
        table_ref[...], rows, (((1,), (1,)), ((), ())), preferred_element_type=jnp.float32
    )
    real, imag = spectra[:bins], spectra[bins:]
    amplitude = jnp.sqrt(real * real + imag * imag)
    edge = jnp.zeros((8, pair * block), jnp.float32)
    padded[0:8, :] = edge
    padded[8 : 8 + bins, :] = amplitude
    padded[8 + bins :, :] = edge
    smooth = padded[8 - SMOOTH : 8 - SMOOTH + bins, :]
    for shift in range(1 - SMOOTH, SMOOTH + 1):
        smooth = smooth + padded[8 + shift : 8 + shift + bins, :]
    mean = jnp.sum(amplitude, axis=0, keepdims=True) * (1.0 / bins)
    level = jnp.maximum(smooth * (1.0 / (2 * SMOOTH + 1)), 0.8 * mean + 1e-06)
    scale = 1.0 / level
    for part, values in enumerate((real * scale, imag * scale)):
        for which in range(pair):
            row = part * segs + step * pair + which
            held[pl.ds(row, bins, stride=2 * segs), :] = values[
                :, which * block : (which + 1) * block
            ]

    @pl.when(step == pl.num_programs(0) - 1)
    def _():
        white_ref[...] = held[...].astype(jnp.bfloat16)


def whiten(traces, table):
    segs, block, samples = traces.shape
    bins = samples // 2
    pair = 2
    return pl.pallas_call(
        functools.partial(whiten_kernel, pair),
        grid=(segs // pair,),
        out_shape=jax.ShapeDtypeStruct((bins * 2 * segs, block), jnp.bfloat16),
        in_specs=[
            pl.BlockSpec((pair, block, samples), lambda i: (i, 0, 0)),
            pl.BlockSpec((2 * bins, samples), lambda i: (0, 0), pipeline_mode=pl.Buffered(1)),
        ],
        out_specs=pl.BlockSpec((bins * 2 * segs, block), lambda i: (0, 0)),
        scratch_shapes=[
            pltpu.VMEM((bins + 16, pair * block), jnp.float32),
            pltpu.VMEM((bins * 2 * segs, block), jnp.float32),
        ],
        compiler_params=pltpu.CompilerParams(vmem_limit_bytes=56 * MIB),
        cost_estimate=pl.CostEstimate(
            flops=2 * segs * block * samples * samples,
            bytes_accessed=2 * samples * samples + 4 * segs * block * samples,
            transcendentals=segs * block * bins,
        ),
        name="whiten",
    )(traces, table)


def skew(matrix):
    rows, _ = matrix.shape
    return pltpu.roll(matrix, rows, 1, stride=1, stride_axis=0)[:, :rows]


def cross_kernel(own_ref, next_ref, flag_ref, ext_ref, stack_ref, held):
    groups, width, depth, block = own_ref.shape
    half = depth // 2
    flags = skew(flag_ref[...] * ext_ref[...])
    down = lax.broadcasted_iota(jnp.int32, (block, block), 0)
    across = lax.broadcasted_iota(jnp.int32, (block, block), 1)
    reverse = jnp.where(down + across == block - 1, 1.0, 0.0).astype(jnp.bfloat16)

    def one(bin_index, carry):
        deep = groups * depth
        own = own_ref[:, bin_index].reshape(deep, block)
        back = jnp.dot(own, reverse, preferred_element_type=jnp.float32)
        split = back.reshape(groups, depth, block)
        turned = jnp.concatenate([split[:, half:], -split[:, :half]], axis=1)
        left = jnp.concatenate([back, turned.reshape(deep, block)], axis=1).astype(jnp.bfloat16)
        right = jnp.concatenate([own, next_ref[:, bin_index].reshape(deep, block)], axis=1)
        sums = lax.dot_general(
            left, right, (((0,), (0,)), ((), ())), preferred_element_type=jnp.float32
        )
        at = pl.ds(pl.multiple_of(bin_index * block, block), block)
        held[0, at, :] = skew(sums[:block]) * flags
        held[1, at, :] = skew(sums[block:]) * flags
        return carry

    lax.fori_loop(0, width, one, 0, unroll=4)
    rows = block // groups
    for part in range(2):
        for row in range(block):
            column = row % rows * block
            stack_ref[row // rows, part, :, column : column + block] = held[
                part, pl.ds(block - 1 - row, width, stride=block), :
            ].astype(jnp.bfloat16)


def cross(own, following, flags, ext_flags):
    groups, width, depth, block = own.shape
    step = 16
    spec = pl.BlockSpec((groups, step, depth, block), lambda i: (0, i, 0, 0))
    rows = block // groups * block
    return pl.pallas_call(
        cross_kernel,
        grid=(width // step,),
        out_shape=jax.ShapeDtypeStruct((groups, 2, width, rows), jnp.bfloat16),
        in_specs=[
            spec,
            spec,
            pl.BlockSpec((block, 1), lambda i: (0, 0)),
            pl.BlockSpec((1, 2 * block), lambda i: (0, 0)),
        ],
        out_specs=pl.BlockSpec((groups, 2, step, rows), lambda i: (0, 0, i, 0)),
        scratch_shapes=[pltpu.VMEM((2, step * block, block), jnp.float32)],
        compiler_params=pltpu.CompilerParams(vmem_limit_bytes=48 * MIB),
        cost_estimate=pl.CostEstimate(
            flops=8 * width * groups * depth * block * block,
            bytes_accessed=4 * own.size + 4 * width * block * block,
            transcendentals=0,
        ),
        name="cross",
    )(own, following, flags[::-1, None], ext_flags[None, :])


def body(traces, live):
    segs, block, samples = traces.shape
    bins = samples // 2
    groups = lax.axis_size("tm")
    width = bins // groups
    table = jnp.asarray(forward_rows(samples, bins))
    inverse = jnp.asarray(inverse_rows(samples, bins, groups, segs * groups))
    flags = live.astype(jnp.bfloat16)
    white = whiten(traces, table).reshape(groups, width, 2 * segs, block)
    own = lax.all_to_all(white, "tm", split_axis=0, concat_axis=0, tiled=True)
    following, next_flags = from_behind((own, flags), "chan", -1)
    ext_flags = jnp.concatenate([flags, next_flags], axis=0).astype(jnp.float32)
    stack = cross(own, following, flags.astype(jnp.float32), ext_flags)
    stack = lax.all_to_all(stack, "tm", split_axis=0, concat_axis=0, tiled=True)
    lagged = lax.dot_general(
        stack.reshape(2 * bins, block // groups * block),
        inverse,
        (((0,), (0,)), ((), ())),
        preferred_element_type=jnp.float32,
    )
    return lagged.astype(jnp.bfloat16).reshape(block // groups, block, samples)


def solution(mesh):
    in_specs = (P("tm", "chan", None), P("chan"))
    out_specs = P(("chan", "tm"), None, None)
    return jax.shard_map(body, mesh=mesh, in_specs=in_specs, out_specs=out_specs, check_vma=False)
```

time: 778 us -> 471 us (0.61); the launches traced: 765 us -> 467 us
  other arithmetic: 213 us -> 0.01 us
  blocking collectives: 96.3 us -> 286 us
  local copies, waits for them, and re-layouts: 155 us -> 0.22 us
  waiting for transfers between devices: 197 us -> 87.7 us
  matrix products: 88.6 us -> 22 us
  Pallas kernels: 0 us -> 66.4 us
  starting transfers between devices: 14.8 us -> 5.22 us
    all_to_all x1 -> x2, blocking collectives: 96.3 us -> 286 us  [the longest x1 189 us: body(): stack = lax.all_to_all(stack, 'tm', split_axis=0, concat_axis=0, tiled=True)]
    dot_general x2 -> x0, other arithmetic: 138 us -> none  [the longest x1 71.1 us: body(): jnp.einsum('rif,fl->ril', lax.all_to_all(stack, 'tm', split_axis=0, conca...]
    all_to_all x1 -> x0, waiting for transfers between devices: 109 us -> none  [body(): lax.all_to_all(stack, 'tm', split_axis=0, concat_axis=2, tiled=True)]
    dot_general x6 -> x1, matrix products: 88.6 us -> 22 us  [body(): lax.dot_general(stack.reshape(2 * bins, block // groups * block), inverse...]
    pallas_call x0 -> x2, Pallas kernels: none -> 66.4 us  [the longest x1 40.7 us: cross(): pl.pallas_call(cross_kernel, grid=(width // step,), out_shape=jax.ShapeDt...]
    reduce_sum x1 -> x0, other arithmetic: 37.4 us -> none  [whiten(): water = 0.8 * jnp.mean(amplitude, axis=-1, keepdims=True) + 1e-06]
    reshape x3 -> x0, local copies, waits for them, and re-layouts: 35.3 us -> none  [band(): return flat.reshape(rows, width + 1, extra)[:, 1:rows + 1, :]]
    pad x3 -> x0, local copies, waits for them, and re-layouts: 26.9 us -> none  [band(): flat = jnp.pad(flat, ((0, rows), (0, 0)))]
  transfers between devices with their start and end apart: 3 -> 2, of which waited for: 2 -> 1; matrix products, arithmetic and copies ran while one was open for 10% -> 0% of each run, Pallas kernels for 0% -> 0%
where the time goes in v1:
time: 471 us; the launch traced here: 467 us
  blocking collectives  286 us (61%)
  waiting for transfers between devices  87.7 us (19%)
  Pallas kernels  66.4 us (14%)
  matrix products  22 us (5%)
  starting transfers between devices  5.22 us (1%)
    all_to_all x1, blocking collectives, body(): stack = lax.all_to_all(stack, 'tm', split_axis=0, concat_axis=0, tiled=True)  189 us
    all_to_all x1, blocking collectives, body(): own = lax.all_to_all(white, 'tm', split_axis=0, concat_axis=0, tiled=True)  96.8 us
    ppermute x2, waiting for transfers between devices, from_behind(): return lax.ppermute(block, axis, route)  87.7 us
    pallas_call x1, Pallas kernels, cross(): pl.pallas_call(cross_kernel, grid=(width // step,), out_shape=jax.ShapeDt...  40.7 us
    pallas_call x1, Pallas kernels, whiten(): pl.pallas_call(functools.partial(whiten_kernel, pair), grid=(segs // pair...  25.6 us
    dot_general x1, matrix products, body(): lax.dot_general(stack.reshape(2 * bins, block // groups * block), inverse...  22 us
  transfers between devices with their start and end apart: 2, of which 1 were waited for; matrix products, arithmetic and copies ran while one was open for 0% of the time, Pallas kernels for 0%

profile of v1, /device:TPU:13, one launch (start us, length us, event | category | flops | bytes accessed | tf_op | source)
XLA Modules:
  0.0 467.2 jit_solution(14468921892824168994)
XLA Ops:
  0.0 25.6 %whiten.1 = bf16[16384,128]{1,0:T(8,128)(2,1)} custom-call(bf16[8,128,2048]{2,1,0:T(8,128)(2,1)} %traces_ref.1, bf16[2048,2048]{1,0:T(8,128)(2,1)} %constant.4.clone.table_ref), custom_call_target="tpu_custom_call" | custom-call | flops 8589934592 | bytes 16777216 | tf_op jit(solution)/shard_map/whiten/pallas_call | solution.py:77
  25.6 0.0 copy-start
  25.6 96.8 %all_to_all.10.own_ref = bf16[8,128,16,128]{3,2,1,0:T(8,128)(2,1)} all-to-all(bf16[8,128,16,128]{3,2,1,0:T(8,128)(2,1)} %bitcast.10), channel_id=1, replica_groups=mesh['chan'=4,'tm'=8] {'tm'}, dimensions={0} | all-to-all | bytes 8388608 | tf_op jit(solution)/shard_map/all_to_all | solution.py:175
  122.4 3.1 collective-permute-start
  125.5 0.0 copy-done
  125.5 2.2 collective-permute-start.1
  127.7 0.1 rev.3
  127.8 0.1 copy.5.flag_ref
  127.9 87.7 %collective-permute-done.1 = bf16[128]{0:T(256)(128)(2,1)S(1)} collective-permute-done((bf16[128]{0:T(256)(128)(2,1)S(1)}, bf16[128]{0:T(256)(128)(2,1)S(1)}, u32[]{:S(2)}, u32[]{:S(2)}) %collective-permute-start.1) | collective-permute-done | bytes 288 | tf_op jit(solution)/shard_map/ppermute | solution.py:20
  215.6 0.0 collective-permute-done.next_ref
  215.6 40.7 %cross.1 = bf16[8,2,128,2048]{3,2,1,0:T(8,128)(2,1)} custom-call(bf16[8,128,16,128]{3,2,1,0:T(8,128)(2,1)} %all_to_all.10.own_ref, bf16[8,128,16,128]{3,2,1,0:T(8,128)(2,1)} %collective-permute-done.next_ref, f32[128,1]{1,0:T(8,128)S(1)} %copy.5.flag_ref, f32[1,256]{1,0:T(1,128)S(1)} %maximum_convert_fusion.ext_ref), custom_call_target="tpu_custom_call" | custom-call | flops 2147483648 | bytes 16777216 | tf_op jit(solution)/shard_map/cross/pallas_call | solution.py:144
  256.3 188.9 %all_to_all.11 = bf16[8,2,128,2048]{3,2,1,0:T(8,128)(2,1)S(1)} all-to-all(bf16[8,2,128,2048]{3,2,1,0:T(8,128)(2,1)} %cross.1), channel_id=1, replica_groups=mesh['chan'=4,'tm'=8] {'tm'}, dimensions={0} | all-to-all | bytes 16777216 | tf_op jit(solution)/shard_map/all_to_all | solution.py:179
  445.2 22.0 %convolution_convert_fusion = bf16[2048,2048]{1,0:T(8,128)(2,1)} fusion(bf16[2048,2048]{1,0:T(8,128)(2,1)S(1)} %bitcast.9, bf16[2048,2048]{1,0:T(8,128)(2,1)} %constant.5.clone), kind=kOutput, calls=%fused_computation | convolution fusion | flops 17184063488 | bytes 25165824 | tf_op jit(solution)/shard_map/dot_general | solution.py:180
  (2 shorter events, 0.0 us)
Async XLA Ops:
  25.6 99.8 %copy-start = (s32[128]{0:T(128)S(1)}, s32[128]{0:T(128)}, u32[]{:S(2)}) copy-start(s32[128]{0:T(128)} %param.5) | copy-start | bytes 1540
  122.4 93.2 %collective-permute-start = (bf16[8,128,16,128]{3,2,1,0:T(8,128)(2,1)}, bf16[8,128,16,128]{3,2,1,0:T(8,128)(2,1)}, u32[]{:S(2)}, u32[]{:S(2)}) collective-permute-start(bf16[8,128,16,128]{3,2,1,0:T(8,128)(2,1)} %all_to_all.10.own_ref), channel_id=1, source_target_pairs={{8,0},{16,8},{24,16},{9,1},{17,9},{25,17},{10,2},{18,10},{26,18},{... | collective-permute-start | bytes 12582920 | tf_op jit(solution)/shard_map/ppermute | solution.py:20
  125.5 90.1 %collective-permute-start.1 = (bf16[128]{0:T(256)(128)(2,1)S(1)}, bf16[128]{0:T(256)(128)(2,1)S(1)}, u32[]{:S(2)}, u32[]{:S(2)}) collective-permute-start(bf16[128]{0:T(256)(128)(2,1)S(1)} %get-tuple-element.7), channel_id=1, source_target_pairs={{8,0},{16,8},{24,16},{9,1},{17,9},{25,17},{10,2},{18,10},{26,18},{... | collective-permute-start | bytes 776 | tf_op jit(solution)/shard_map/ppermute | solution.py:20

commit v2 on v1

v2 whole, which is shorter than its diff:
```python
import functools
import math

import jax
import jax.numpy as jnp
import ml_dtypes
import numpy as np
from jax import lax
from jax.experimental import pallas as pl
from jax.experimental.pallas import tpu as pltpu
from jax.sharding import PartitionSpec as P

SMOOTH = 4
MIB = 1 << 20
CHUNKS = 4


def from_behind(block, axis, distance):
    devices = range(lax.axis_size(axis))
    route = [(i - distance, i) for i in devices if i - distance in devices]
    return lax.ppermute(block, axis, route)


def forward_rows(samples, bins):
    phase = np.outer(np.arange(bins), np.arange(samples)) % samples
    angle = phase * (2.0 * math.pi / samples)
    return np.concatenate([np.cos(angle), -np.sin(angle)], axis=0).astype(ml_dtypes.bfloat16)


def inverse_rows(samples, bins, groups, segments):
    lag = np.arange(samples) - samples // 2
    phase = np.mod(np.outer(np.arange(bins), lag), samples)
    angle = phase * (2.0 * math.pi / samples)
    weight = np.where(np.arange(bins) == 0, 1.0, 2.0)[:, None] / math.sqrt(samples * segments)
    width = bins // groups
    wave = np.stack([weight * np.cos(angle), -weight * np.sin(angle)])
    wave = wave.reshape(2, groups, width, samples).transpose(1, 0, 2, 3)
    return wave.reshape(2 * bins, samples).astype(ml_dtypes.bfloat16)


def whiten_kernel(pair, traces_ref, table_ref, white_ref, padded, held):
    _, block, samples = traces_ref.shape
    bins = samples // 2
    segs = held.shape[0] // bins // 2
    step = pl.program_id(0)
    rows = traces_ref[...].reshape(pair * block, samples)
    spectra = lax.dot_general(
        table_ref[...], rows, (((1,), (1,)), ((), ())), preferred_element_type=jnp.float32
    )
    real, imag = spectra[:bins], spectra[bins:]
    amplitude = jnp.sqrt(real * real + imag * imag)
    edge = jnp.zeros((8, pair * block), jnp.float32)
    padded[0:8, :] = edge
    padded[8 : 8 + bins, :] = amplitude
    padded[8 + bins :, :] = edge
    smooth = padded[8 - SMOOTH : 8 - SMOOTH + bins, :]
    for shift in range(1 - SMOOTH, SMOOTH + 1):
        smooth = smooth + padded[8 + shift : 8 + shift + bins, :]
    mean = jnp.sum(amplitude, axis=0, keepdims=True) * (1.0 / bins)
    level = jnp.maximum(smooth * (1.0 / (2 * SMOOTH + 1)), 0.8 * mean + 1e-06)
    scale = 1.0 / level
    for part, values in enumerate((real * scale, imag * scale)):
        for which in range(pair):
            row = part * segs + step * pair + which
            held[pl.ds(row, bins, stride=2 * segs), :] = values[
                :, which * block : (which + 1) * block
            ]

    @pl.when(step == pl.num_programs(0) - 1)
    def _():
        chunks, groups, rows, _ = white_ref.shape
        for group in range(groups):
            for chunk in range(chunks):
                first = (group * chunks + chunk) * rows
                white_ref[chunk, group] = held[first : first + rows, :].astype(jnp.bfloat16)


def whiten(traces, table, groups):
    segs, block, samples = traces.shape
    bins = samples // 2
    pair = 2
    rows = bins // groups // CHUNKS * 2 * segs
    return pl.pallas_call(
        functools.partial(whiten_kernel, pair),
        grid=(segs // pair,),
        out_shape=jax.ShapeDtypeStruct((CHUNKS, groups, rows, block), jnp.bfloat16),
        in_specs=[
            pl.BlockSpec((pair, block, samples), lambda i: (i, 0, 0)),
            pl.BlockSpec((2 * bins, samples), lambda i: (0, 0), pipeline_mode=pl.Buffered(1)),
        ],
        out_specs=pl.BlockSpec((CHUNKS, groups, rows, block), lambda i: (0, 0, 0, 0)),
        scratch_shapes=[
            pltpu.VMEM((bins + 16, pair * block), jnp.float32),
            pltpu.VMEM((bins * 2 * segs, block), jnp.float32),
        ],
        compiler_params=pltpu.CompilerParams(vmem_limit_bytes=56 * MIB),
        cost_estimate=pl.CostEstimate(
            flops=2 * segs * block * samples * samples,
            bytes_accessed=2 * samples * samples + 4 * segs * block * samples,
            transcendentals=segs * block * bins,
        ),
        name="whiten",
    )(traces, table)


def skew(matrix):
    rows, _ = matrix.shape
    return pltpu.roll(matrix, rows, 1, stride=1, stride_axis=0)[:, :rows]


def cross_chunk(own, following, flags, reverse, held, stack):
    groups, width, depth, block = own.shape
    half = depth // 2
    deep = groups * depth

    def one(bin_index, carry):
        mine = own[:, bin_index].reshape(deep, block)
        back = jnp.dot(mine, reverse, preferred_element_type=jnp.float32)
        split = back.reshape(groups, depth, block)
        turned = jnp.concatenate([split[:, half:], -split[:, :half]], axis=1)
        left = jnp.concatenate([back, turned.reshape(deep, block)], axis=1).astype(jnp.bfloat16)
        right = jnp.concatenate([mine, following[:, bin_index].reshape(deep, block)], axis=1)
        sums = lax.dot_general(
            left, right, (((0,), (0,)), ((), ())), preferred_element_type=jnp.float32
        )
        at = pl.ds(pl.multiple_of(bin_index * block, block), block)
        held[0, at, :] = skew(sums[:block]) * flags
        held[1, at, :] = skew(sums[block:]) * flags
        return carry

    lax.fori_loop(0, width, one, 0, unroll=4)
    rows = block // groups

    def spread(row, carry):
        column = pl.ds(pl.multiple_of(row * block, block), block)
        for group in range(groups):
            first = block - 1 - group * rows - row
            for part in range(2):
                stack[group, part, :, column] = held[
                    part, pl.ds(first, width, stride=block), :
                ].astype(jnp.bfloat16)
        return carry

    lax.fori_loop(0, rows, spread, 0)


def exchange_kernel(
    n_chan,
    white_ref,
    flag_ref,
    ext_ref,
    result_ref,
    own,
    following,
    stack,
    held,
    first_send,
    first_recv,
    shift_send,
    shift_recv,
    last_send,
    last_recv,
    local_sem,
):
    chunks, groups, _, _, block = own.shape
    me = lax.axis_index("tm")
    place = lax.axis_index("chan")
    before = lax.rem(place + n_chan - 1, n_chan)
    after = lax.rem(place + 1, n_chan)
    middle = groups // 2
    order = sorted(range(1, groups), key=lambda distance: abs(distance - middle))
    peers = [lax.rem(me + distance, groups) for distance in order]

    def first(chunk, peer, slot):
        return pltpu.make_async_remote_copy(
            src_ref=white_ref.at[chunk, peer],
            dst_ref=own.at[chunk, slot],
            send_sem=first_send.at[chunk, peer],
            recv_sem=first_recv.at[chunk, slot],
            device_id={"tm": peer},
            device_id_type=pl.DeviceIdType.MESH,
        )

    def shift(chunk):
        return pltpu.make_async_remote_copy(
            src_ref=own.at[chunk],
            dst_ref=following.at[chunk],
            send_sem=shift_send.at[chunk],
            recv_sem=shift_recv.at[chunk],
            device_id={"chan": before},
            device_id_type=pl.DeviceIdType.MESH,
        )

    def last(chunk, peer, slot):
        return pltpu.make_async_remote_copy(
            src_ref=stack.at[chunk, peer],
            dst_ref=result_ref.at[chunk, slot],
            send_sem=last_send.at[chunk, peer],
            recv_sem=last_recv.at[chunk, slot],
            device_id={"tm": peer},
            device_id_type=pl.DeviceIdType.MESH,
        )

    def keep_white(chunk):
        return pltpu.make_async_copy(
            white_ref.at[chunk, me], own.at[chunk, me], local_sem.at[0, chunk]
        )

    def keep_stack(chunk):
        return pltpu.make_async_copy(
            stack.at[chunk, me], result_ref.at[chunk, me], local_sem.at[1, chunk]
        )

    barrier = pltpu.get_barrier_semaphore()
    for peer in peers:
        pl.semaphore_signal(
            barrier, inc=1, device_id={"tm": peer}, device_id_type=pl.DeviceIdType.MESH
        )
    for neighbour in (before, after):
        pl.semaphore_signal(
            barrier, inc=1, device_id={"chan": neighbour}, device_id_type=pl.DeviceIdType.MESH
        )
    pl.semaphore_wait(barrier, groups + 1)

    def start_first(chunk):
        for peer in peers:
            first(chunk, peer, me).start()
        keep_white(chunk).start()

    def arrive(chunk):
        for peer in peers:
            first(chunk, peer, peer).wait_recv()
        keep_white(chunk).wait()
        shift(chunk).start()

    def work(chunk):
        shift(chunk).wait_recv()
        cross_chunk(own.at[chunk], following.at[chunk], flags, reverse, held, stack.at[chunk])
        for peer in peers:
            last(chunk, peer, me).start()
        keep_stack(chunk).start()

    start_first(0)
    start_first(1)
    flags = skew(flag_ref[...] * ext_ref[...])
    down = lax.broadcasted_iota(jnp.int32, (block, block), 0)
    across = lax.broadcasted_iota(jnp.int32, (block, block), 1)
    reverse = jnp.where(down + across == block - 1, 1.0, 0.0).astype(jnp.bfloat16)
    for chunk in range(chunks):
        arrive(chunk)
        if chunk + 2 < chunks:
            start_first(chunk + 2)
        if chunk >= 1:
            work(chunk - 1)
    work(chunks - 1)
    for chunk in range(chunks):
        for peer in peers:
            first(chunk, peer, peer).wait_send()
            last(chunk, peer, peer).wait_send()
            last(chunk, peer, peer).wait_recv()
        shift(chunk).wait_send()
        keep_stack(chunk).wait()


def exchange(white, flags, ext_flags):
    chunks, groups, width, depth, block = white.shape
    rows = block // groups * block
    stack = (chunks, groups, 2, width, rows)
    dma = pltpu.SemaphoreType.DMA
    return pl.pallas_call(
        functools.partial(exchange_kernel, lax.axis_size("chan")),
        out_shape=jax.ShapeDtypeStruct(stack, jnp.bfloat16),
        in_specs=[
            pl.BlockSpec(memory_space=pl.ANY),
            pl.BlockSpec(memory_space=pltpu.VMEM),
            pl.BlockSpec(memory_space=pltpu.VMEM),
        ],
        out_specs=pl.BlockSpec(memory_space=pl.ANY),
        scratch_shapes=[
            pltpu.VMEM(white.shape, jnp.bfloat16),
            pltpu.VMEM(white.shape, jnp.bfloat16),
            pltpu.VMEM(stack, jnp.bfloat16),
            pltpu.VMEM((2, width * block, block), jnp.float32),
            dma((chunks, groups)),
            dma((chunks, groups)),
            dma((chunks,)),
            dma((chunks,)),
            dma((chunks, groups)),
            dma((chunks, groups)),
            dma((2, chunks)),
        ],
        compiler_params=pltpu.CompilerParams(
            vmem_limit_bytes=52 * MIB, collective_id=0, has_side_effects=True
        ),
        cost_estimate=pl.CostEstimate(
            flops=8 * chunks * width * groups * depth * block * block,
            bytes_accessed=8 * white.size,
            transcendentals=0,
        ),
        name="exchange",
    )(white, flags[::-1, None], ext_flags[None, :])


def body(traces, live):
    segs, block, samples = traces.shape
    bins = samples // 2
    groups = lax.axis_size("tm")
    width = bins // groups
    table = jnp.asarray(forward_rows(samples, bins))
    inverse = inverse_rows(samples, bins, groups, segs * groups)
    inverse = inverse.reshape(groups, 2, CHUNKS, width // CHUNKS, samples)
    inverse = inverse.transpose(2, 0, 1, 3, 4).reshape(2 * bins, samples)
    flags = live.astype(jnp.bfloat16)
    next_flags = from_behind(flags, "chan", -1)
    ext_flags = jnp.concatenate([flags, next_flags], axis=0).astype(jnp.float32)
    own_flags = flags.astype(jnp.float32)
    part = width // CHUNKS
    white = whiten(traces, table, groups).reshape(CHUNKS, groups, part, 2 * segs, block)
    stack = exchange(white, own_flags, ext_flags)
    lagged = lax.dot_general(
        stack.reshape(2 * bins, block // groups * block),
        jnp.asarray(inverse),
        (((0,), (0,)), ((), ())),
        preferred_element_type=jnp.float32,
    )
    return lagged.astype(jnp.bfloat16).reshape(block // groups, block, samples)


def solution(mesh):
    in_specs = (P("tm", "chan", None), P("chan"))
    out_specs = P(("chan", "tm"), None, None)
    return jax.shard_map(body, mesh=mesh, in_specs=in_specs, out_specs=out_specs, check_vma=False)
```

time: 471 us -> 329 us (0.70)
  blocking collectives: 286 us -> 0 us
  Pallas kernels: 66.4 us -> 302 us
  waiting for transfers between devices: 87.7 us -> 0.01 us
    all_to_all x2 -> x0, blocking collectives: 286 us -> none  [the longest x1 189 us: body(): stack = lax.all_to_all(stack, 'tm', split_axis=0, concat_axis=0, tiled=True)]
    pallas_call x1, Pallas kernels: 40.7 us -> 276 us  [exchange(): pl.pallas_call(functools.partial(exchange_kernel, lax.axis_size('chan')),...]
    ppermute x2 -> x1, waiting for transfers between devices: 87.7 us -> 0.01 us  [from_behind(): return lax.ppermute(block, axis, route)]
  transfers between devices with their start and end apart: 2 -> 1, of which waited for: 1 -> 0; matrix products, arithmetic and copies ran while one was open for 0% -> 0% of each run, Pallas kernels for 0% -> 8%
where the time goes in v2:
time: 329 us
  Pallas kernels  302 us (92%)
  matrix products  23.9 us (7%)
    pallas_call x1, Pallas kernels, exchange(): pl.pallas_call(functools.partial(exchange_kernel, lax.axis_size('chan')),...  276 us
    pallas_call x1, Pallas kernels, whiten(): pl.pallas_call(functools.partial(whiten_kernel, pair), grid=(segs // pair...  25.7 us
    dot_general x1, matrix products, body(): lax.dot_general(stack.reshape(2 * bins, block // groups * block), jnp.asa...  23.9 us
  transfers between devices with their start and end apart: 1, of which 0 were waited for; matrix products, arithmetic and copies ran while one was open for 0% of the time, Pallas kernels for 8%

profile of v2, /device:TPU:13, one launch (start us, length us, event | category | flops | bytes accessed | tf_op | source)
XLA Modules:
  0.0 329.3 jit_solution(17064742585668176959)
XLA Ops:
  0.0 0.7 convert_bitcast_fusion
  0.7 3.0 collective-permute-start
  3.7 25.7 %whiten.1 = bf16[4,8,512,128]{3,2,1,0:T(8,128)(2,1)} custom-call(bf16[8,128,2048]{2,1,0:T(8,128)(2,1)} %traces_ref.1, bf16[2048,2048]{1,0:T(8,128)(2,1)} %constant.4.clone.table_ref), custom_call_target="tpu_custom_call" | custom-call | flops 8589934592 | bytes 16777216 | tf_op jit(solution)/shard_map/whiten/pallas_call | solution.py:83
  29.4 0.1 rev.3
  29.5 0.1 copy.5.flag_ref
  29.6 0.0 collective-permute-done
  29.6 275.9 %exchange.1 = bf16[4,8,2,32,2048]{4,3,2,1,0:T(8,128)(2,1)} custom-call(bf16[4,8,32,16,128]{4,3,2,1,0:T(8,128)(2,1)} %bitcast.10, f32[128,1]{1,0:T(8,128)S(1)} %copy.5.flag_ref, f32[1,256]{1,0:T(1,128)S(1)} %maximum_convert_fusion.ext_ref), custom_call_target="tpu_custom_call" | custom-call | flops 2147483648 | bytes 16777216 | tf_op jit(solution)/shard_map/exchange/pallas_call | solution.py:270
  305.5 23.9 %convolution_convert_fusion = bf16[2048,2048]{1,0:T(8,128)(2,1)} fusion(bf16[2048,2048]{1,0:T(8,128)(2,1)} %bitcast.9, bf16[2048,2048]{1,0:T(8,128)(2,1)} %constant.5.clone), kind=kOutput, calls=%fused_computation | convolution fusion | flops 17184063488 | bytes 25165824 | tf_op jit(solution)/shard_map/dot_general | solution.py:320
  (1 shorter events, 0.0 us)
Async XLA Ops:
  0.7 28.9 %collective-permute-start = (bf16[128]{0:T(256)(128)(2,1)S(1)}, bf16[128]{0:T(256)(128)(2,1)S(1)}, u32[]{:S(2)}, u32[]{:S(2)}) collective-permute-start(bf16[128]{0:T(256)(128)(2,1)S(1)} %get-tuple-element.7), channel_id=1, source_target_pairs={{8,0},{16,8},{24,16},{9,1},{17,9},{25,17},{10,2},{18,10},{26,18},{... | collective-permute-start | bytes 776 | tf_op jit(solution)/shard_map/ppermute | solution.py:21

commit v3 on v2

--- a/solution.py
+++ b/solution.py
@@ -12,7 +12,8 @@
 
 SMOOTH = 4
 MIB = 1 << 20
-CHUNKS = 4
+CHUNKS = 8
+SPANS = 2
 
 
 def from_behind(block, axis, distance):
@@ -103,45 +104,47 @@
     )(traces, table)
 
 
-def skew(matrix):
-    rows, _ = matrix.shape
-    return pltpu.roll(matrix, rows, 1, stride=1, stride_axis=0)[:, :rows]
-
-
-def cross_chunk(own, following, flags, reverse, held, stack):
+def skew(matrix, shift, columns):
+    return pltpu.roll(matrix, shift, 1, stride=1, stride_axis=0)[:, :columns]
+
+
+def cross_chunk(own, following, flags, shift, reverse, held, stack):
     groups, width, depth, block = own.shape
+    members = stack.shape[0]
+    rows = held.shape[1] // width
+    share = rows // members
     half = depth // 2
     deep = groups * depth
+    lane = lax.broadcasted_iota(jnp.int32, (1, 1, 2 * rows), 2)
 
     def one(bin_index, carry):
         mine = own[:, bin_index].reshape(deep, block)
         back = jnp.dot(mine, reverse, preferred_element_type=jnp.float32)
-        split = back.reshape(groups, depth, block)
-        turned = jnp.concatenate([split[:, half:], -split[:, :half]], axis=1)
-        left = jnp.concatenate([back, turned.reshape(deep, block)], axis=1).astype(jnp.bfloat16)
+        back = back.reshape(groups, depth, 2 * rows)
+        turned = jnp.concatenate([back[:, half:], -back[:, :half]], axis=1)
+        left = jnp.where(lane < rows, back, turned).reshape(deep, 2 * rows).astype(jnp.bfloat16)
         right = jnp.concatenate([mine, following[:, bin_index].reshape(deep, block)], axis=1)
         sums = lax.dot_general(
             left, right, (((0,), (0,)), ((), ())), preferred_element_type=jnp.float32
         )
-        at = pl.ds(pl.multiple_of(bin_index * block, block), block)
-        held[0, at, :] = skew(sums[:block]) * flags
-        held[1, at, :] = skew(sums[block:]) * flags
+        at = pl.ds(pl.multiple_of(bin_index * rows, rows), rows)
+        held[0, at, :] = skew(sums[:rows], shift, block) * flags
+        held[1, at, :] = skew(sums[rows:], shift, block) * flags
         return carry
 
     lax.fori_loop(0, width, one, 0, unroll=4)
-    rows = block // groups
 
     def spread(row, carry):
         column = pl.ds(pl.multiple_of(row * block, block), block)
-        for group in range(groups):
-            first = block - 1 - group * rows - row
+        for member in range(members):
+            first = rows - 1 - member * share - row
             for part in range(2):
-                stack[group, part, :, column] = held[
-                    part, pl.ds(first, width, stride=block), :
+                stack[member, part, :, column] = held[
+                    part, pl.ds(first, width, stride=rows), :
                 ].astype(jnp.bfloat16)
         return carry
 
-    lax.fori_loop(0, rows, spread, 0)
+    lax.fori_loop(0, share, spread, 0)
 
 
 def exchange_kernel(
@@ -162,7 +165,9 @@
     last_recv,
     local_sem,
 ):
-    chunks, groups, _, _, block = own.shape
+    chunks, groups, width, _, block = own.shape
+    members = groups // SPANS
+    rows = block // SPANS
     me = lax.axis_index("tm")
     place = lax.axis_index("chan")
     before = lax.rem(place + n_chan - 1, n_chan)
@@ -170,10 +175,13 @@
     middle = groups // 2
     order = sorted(range(1, groups), key=lambda distance: abs(distance - middle))
     peers = [lax.rem(me + distance, groups) for distance in order]
+    span = me // members
+    mine = lax.rem(me, members)
+    mates = [lax.rem(mine + distance, members) for distance in range(1, members)]
 
     def first(chunk, peer, slot):
         return pltpu.make_async_remote_copy(
-            src_ref=white_ref.at[chunk, peer],
+            src_ref=white_ref.at[chunk, lax.rem(peer, members)],
             dst_ref=own.at[chunk, slot],
             send_sem=first_send.at[chunk, peer],
             recv_sem=first_recv.at[chunk, slot],
@@ -191,24 +199,24 @@
             device_id_type=pl.DeviceIdType.MESH,
         )
 
-    def last(chunk, peer, slot):
+    def last(chunk, mate, slot):
         return pltpu.make_async_remote_copy(
-            src_ref=stack.at[chunk, peer],
+            src_ref=stack.at[chunk, mate],
             dst_ref=result_ref.at[chunk, slot],
-            send_sem=last_send.at[chunk, peer],
+            send_sem=last_send.at[chunk, mate],
             recv_sem=last_recv.at[chunk, slot],
-            device_id={"tm": peer},
+            device_id={"tm": span * members + mate},
             device_id_type=pl.DeviceIdType.MESH,
         )
 
     def keep_white(chunk):
         return pltpu.make_async_copy(
-            white_ref.at[chunk, me], own.at[chunk, me], local_sem.at[0, chunk]
+            white_ref.at[chunk, mine], own.at[chunk, me], local_sem.at[0, chunk]
         )
 
     def keep_stack(chunk):
         return pltpu.make_async_copy(
-            stack.at[chunk, me], result_ref.at[chunk, me], local_sem.at[1, chunk]
+            stack.at[chunk, mine], result_ref.at[chunk, mine], local_sem.at[1, chunk]
         )
 
     barrier = pltpu.get_barrier_semaphore()
@@ -235,17 +243,25 @@
 
     def work(chunk):
         shift(chunk).wait_recv()
-        cross_chunk(own.at[chunk], following.at[chunk], flags, reverse, held, stack.at[chunk])
-        for peer in peers:
-            last(chunk, peer, me).start()
+        for which in range(SPANS):
+
+            @pl.when(span == which)
+            def _():
+                turn = 2 * block - (which + 1) * rows
+                flags = skew(flag_ref[...] * ext_ref[...], turn, block)
+                cross_chunk(
+                    own.at[chunk], following.at[chunk], flags, turn, reverse, held, stack.at[chunk]
+                )
+
+        for mate in mates:
+            last(chunk, mate, mine).start()
         keep_stack(chunk).start()
 
     start_first(0)
     start_first(1)
-    flags = skew(flag_ref[...] * ext_ref[...])
-    down = lax.broadcasted_iota(jnp.int32, (block, block), 0)
-    across = lax.broadcasted_iota(jnp.int32, (block, block), 1)
-    reverse = jnp.where(down + across == block - 1, 1.0, 0.0).astype(jnp.bfloat16)
+    down = lax.broadcasted_iota(jnp.int32, (block, 2 * rows), 0)
+    across = lax.broadcasted_iota(jnp.int32, (block, 2 * rows), 1) % rows
+    reverse = jnp.where(down + across == (span + 1) * rows - 1, 1.0, 0.0).astype(jnp.bfloat16)
     for chunk in range(chunks):
         arrive(chunk)
         if chunk + 2 < chunks:
@@ -256,16 +272,18 @@
     for chunk in range(chunks):
         for peer in peers:
             first(chunk, peer, peer).wait_send()
-            last(chunk, peer, peer).wait_send()
-            last(chunk, peer, peer).wait_recv()
+        for mate in mates:
+            last(chunk, mate, mate).wait_send()
+            last(chunk, mate, mate).wait_recv()
         shift(chunk).wait_send()
         keep_stack(chunk).wait()
 
 
 def exchange(white, flags, ext_flags):
-    chunks, groups, width, depth, block = white.shape
-    rows = block // groups * block
-    stack = (chunks, groups, 2, width, rows)
+    chunks, members, width, depth, block = white.shape
+    groups = members * SPANS
+    gathered = (chunks, groups, width, depth, block)
+    stack = (chunks, members, 2, width, block // groups * block)
     dma = pltpu.SemaphoreType.DMA
     return pl.pallas_call(
         functools.partial(exchange_kernel, lax.axis_size("chan")),
@@ -277,16 +295,16 @@
         ],
         out_specs=pl.BlockSpec(memory_space=pl.ANY),
         scratch_shapes=[
-            pltpu.VMEM(white.shape, jnp.bfloat16),
-            pltpu.VMEM(white.shape, jnp.bfloat16),
+            pltpu.VMEM(gathered, jnp.bfloat16),
+            pltpu.VMEM(gathered, jnp.bfloat16),
             pltpu.VMEM(stack, jnp.bfloat16),
-            pltpu.VMEM((2, width * block, block), jnp.float32),
+            pltpu.VMEM((2, width * (block // SPANS), block), jnp.float32),
             dma((chunks, groups)),
             dma((chunks, groups)),
             dma((chunks,)),
             dma((chunks,)),
-            dma((chunks, groups)),
-            dma((chunks, groups)),
+            dma((chunks, members)),
+            dma((chunks, members)),
             dma((2, chunks)),
         ],
         compiler_params=pltpu.CompilerParams(
@@ -294,29 +312,31 @@
         ),
         cost_estimate=pl.CostEstimate(
             flops=8 * chunks * width * groups * depth * block * block,
-            bytes_accessed=8 * white.size,
+            bytes_accessed=12 * white.size,
             transcendentals=0,
         ),
         name="exchange",
-    )(white, flags[::-1, None], ext_flags[None, :])
+    )(white, flags[:, None], ext_flags[None, :])
 
 
 def body(traces, live):
     segs, block, samples = traces.shape
     bins = samples // 2
     groups = lax.axis_size("tm")
-    width = bins // groups
+    members = groups // SPANS
+    part = bins // members // CHUNKS
     table = jnp.asarray(forward_rows(samples, bins))
-    inverse = inverse_rows(samples, bins, groups, segs * groups)
-    inverse = inverse.reshape(groups, 2, CHUNKS, width // CHUNKS, samples)
+    inverse = inverse_rows(samples, bins, members, segs * groups)
+    inverse = inverse.reshape(members, 2, CHUNKS, part, samples)
     inverse = inverse.transpose(2, 0, 1, 3, 4).reshape(2 * bins, samples)
     flags = live.astype(jnp.bfloat16)
     next_flags = from_behind(flags, "chan", -1)
     ext_flags = jnp.concatenate([flags, next_flags], axis=0).astype(jnp.float32)
-    own_flags = flags.astype(jnp.float32)
-    part = width // CHUNKS
-    white = whiten(traces, table, groups).reshape(CHUNKS, groups, part, 2 * segs, block)
-    stack = exchange(white, own_flags, ext_flags)
+    rows = block // SPANS
+    span = lax.axis_index("tm") // members
+    span_flags = lax.dynamic_slice(flags.astype(jnp.float32), (span * rows,), (rows,))[::-1]
+    white = whiten(traces, table, members).reshape(CHUNKS, members, part, 2 * segs, block)
+    stack = exchange(white, span_flags, ext_flags)
     lagged = lax.dot_general(
         stack.reshape(2 * bins, block // groups * block),
         jnp.asarray(inverse),

time: 329 us -> 302 us (0.918)
  Pallas kernels: 302 us -> 272 us
    pallas_call x1, Pallas kernels: 276 us -> 246 us  [exchange(): pl.pallas_call(functools.partial(exchange_kernel, lax.axis_size('chan')),...]
  transfers between devices with their start and end apart: 1 -> 1, of which waited for: 0 -> 0; matrix products, arithmetic and copies ran while one was open for 0% -> 0% of each run, Pallas kernels for 8% -> 9%
where the time goes in v3:
time: 302 us; the launch traced here: 299 us
  Pallas kernels  272 us (90%)
  matrix products  23.7 us (8%)
  starting transfers between devices  3.05 us (1%)
    pallas_call x1, Pallas kernels, exchange(): pl.pallas_call(functools.partial(exchange_kernel, lax.axis_size('chan')),...  246 us
    pallas_call x1, Pallas kernels, whiten(): pl.pallas_call(functools.partial(whiten_kernel, pair), grid=(segs // pair...  25.7 us
    dot_general x1, matrix products, body(): lax.dot_general(stack.reshape(2 * bins, block // groups * block), jnp.asa...  23.7 us
  transfers between devices with their start and end apart: 1, of which 0 were waited for; matrix products, arithmetic and copies ran while one was open for 0% of the time, Pallas kernels for 9%

profile of v3, /device:TPU:13, one launch (start us, length us, event | category | flops | bytes accessed | tf_op | source)
XLA Modules:
  0.0 299.4 jit_solution(1147158973504807273)
XLA Ops:
  0.0 0.7 convert_bitcast_fusion
  0.7 3.0 %collective-permute-start = (bf16[128]{0:T(256)(128)(2,1)S(1)}, bf16[128]{0:T(256)(128)(2,1)S(1)}, u32[]{:S(2)}, u32[]{:S(2)}) collective-permute-start(bf16[128]{0:T(256)(128)(2,1)S(1)} %get-tuple-element.7), channel_id=1, source_target_pairs={{8,0},{16,8},{24,16},{9,1},{17,9},{25,17},{10,2},{18,10},{26,18},{... | collective-permute-start | bytes 776 | tf_op jit(solution)/shard_map/ppermute | solution.py:22
  3.7 25.7 %whiten.1 = bf16[8,4,512,128]{3,2,1,0:T(8,128)(2,1)} custom-call(bf16[8,128,2048]{2,1,0:T(8,128)(2,1)} %traces_ref.1, bf16[2048,2048]{1,0:T(8,128)(2,1)} %constant.29.clone.table_ref), custom_call_target="tpu_custom_call" | custom-call | flops 8589934592 | bytes 16777216 | tf_op jit(solution)/shard_map/whiten/pallas_call | solution.py:84
  29.4 0.1 dynamic_slice.3
  29.5 0.1 rev.3
  29.6 0.1 copy.5.flag_ref
  29.7 0.0 collective-permute-done
  29.7 246.1 %exchange.1 = bf16[8,4,2,32,2048]{4,3,2,1,0:T(8,128)(2,1)} custom-call(bf16[8,4,32,16,128]{4,3,2,1,0:T(8,128)(2,1)} %bitcast.12, f32[64,1]{1,0:T(8,128)S(1)} %copy.5.flag_ref, f32[1,256]{1,0:T(1,128)S(1)} %maximum_convert_fusion.ext_ref), custom_call_target="tpu_custom_call" | custom-call | flops 4294967296 | bytes 25165824 | tf_op jit(solution)/shard_map/exchange/pallas_call | solution.py:288
  275.7 23.7 %convolution_convert_fusion = bf16[2048,2048]{1,0:T(8,128)(2,1)} fusion(bf16[2048,2048]{1,0:T(8,128)(2,1)} %bitcast.11, bf16[2048,2048]{1,0:T(8,128)(2,1)} %constant.30.clone), kind=kOutput, calls=%fused_computation | convolution fusion | flops 17184063488 | bytes 25165824 | tf_op jit(solution)/shard_map/dot_general | solution.py:340
  (1 shorter events, 0.0 us)
Async XLA Ops:
  0.7 29.0 %collective-permute-start = (bf16[128]{0:T(256)(128)(2,1)S(1)}, bf16[128]{0:T(256)(128)(2,1)S(1)}, u32[]{:S(2)}, u32[]{:S(2)}) collective-permute-start(bf16[128]{0:T(256)(128)(2,1)S(1)} %get-tuple-element.7), channel_id=1, source_target_pairs={{8,0},{16,8},{24,16},{9,1},{17,9},{25,17},{10,2},{18,10},{26,18},{... | collective-permute-start | bytes 776 | tf_op jit(solution)/shard_map/ppermute | solution.py:22

commit v4 on v3

--- a/solution.py
+++ b/solution.py
@@ -12,8 +12,9 @@
 
 SMOOTH = 4
 MIB = 1 << 20
-CHUNKS = 8
+PART = 16
 SPANS = 2
+AHEAD = 3
 
 
 def from_behind(block, axis, distance):
@@ -39,35 +40,49 @@
     return wave.reshape(2 * bins, samples).astype(ml_dtypes.bfloat16)
 
 
-def whiten_kernel(pair, traces_ref, table_ref, white_ref, padded, held):
-    _, block, samples = traces_ref.shape
+def whiten_kernel(pair, traces_ref, table_ref, white_ref, spectra, padded, held):
+    count, block, samples = traces_ref.shape
     bins = samples // 2
     segs = held.shape[0] // bins // 2
-    step = pl.program_id(0)
-    rows = traces_ref[...].reshape(pair * block, samples)
-    spectra = lax.dot_general(
-        table_ref[...], rows, (((1,), (1,)), ((), ())), preferred_element_type=jnp.float32
-    )
-    real, imag = spectra[:bins], spectra[bins:]
-    amplitude = jnp.sqrt(real * real + imag * imag)
-    edge = jnp.zeros((8, pair * block), jnp.float32)
-    padded[0:8, :] = edge
-    padded[8 : 8 + bins, :] = amplitude
-    padded[8 + bins :, :] = edge
-    smooth = padded[8 - SMOOTH : 8 - SMOOTH + bins, :]
-    for shift in range(1 - SMOOTH, SMOOTH + 1):
-        smooth = smooth + padded[8 + shift : 8 + shift + bins, :]
-    mean = jnp.sum(amplitude, axis=0, keepdims=True) * (1.0 / bins)
-    level = jnp.maximum(smooth * (1.0 / (2 * SMOOTH + 1)), 0.8 * mean + 1e-06)
-    scale = 1.0 / level
-    for part, values in enumerate((real * scale, imag * scale)):
-        for which in range(pair):
-            row = part * segs + step * pair + which
-            held[pl.ds(row, bins, stride=2 * segs), :] = values[
-                :, which * block : (which + 1) * block
-            ]
-
-    @pl.when(step == pl.num_programs(0) - 1)
+    lanes = pair * block
+    origin = pl.program_id(0) * count
+    edge = jnp.zeros((8, lanes), jnp.float32)
+    for slot in range(2):
+        padded[slot, 0:8, :] = edge
+        padded[slot, 8 + bins :, :] = edge
+
+    def transform(step):
+        rows = traces_ref[step * pair : (step + 1) * pair].reshape(lanes, samples)
+        spectra[step % 2] = lax.dot_general(
+            table_ref[...], rows, (((1,), (1,)), ((), ())), preferred_element_type=jnp.float32
+        )
+
+    def finish(step):
+        slot = step % 2
+        real, imag = spectra[slot, :bins], spectra[slot, bins:]
+        amplitude = jnp.sqrt(real * real + imag * imag)
+        padded[slot, 8 : 8 + bins, :] = amplitude
+        smooth = padded[slot, 8 - SMOOTH : 8 - SMOOTH + bins, :]
+        for shift in range(1 - SMOOTH, SMOOTH + 1):
+            smooth = smooth + padded[slot, 8 + shift : 8 + shift + bins, :]
+        mean = jnp.sum(amplitude, axis=0, keepdims=True) * (1.0 / bins)
+        level = jnp.maximum(smooth * (1.0 / (2 * SMOOTH + 1)), 0.8 * mean + 1e-06)
+        scale = 1.0 / level
+        for part, values in enumerate((real * scale, imag * scale)):
+            for which in range(pair):
+                row = part * segs + origin + step * pair + which
+                held[pl.ds(row, bins, stride=2 * segs), :] = values[
+                    :, which * block : (which + 1) * block
+                ]
+
+    steps = count // pair
+    transform(0)
+    for step in range(steps):
+        if step + 1 < steps:
+            transform(step + 1)
+        finish(step)
+
+    @pl.when(pl.program_id(0) == pl.num_programs(0) - 1)
     def _():
         chunks, groups, rows, _ = white_ref.shape
         for group in range(groups):
@@ -80,18 +95,20 @@
     segs, block, samples = traces.shape
     bins = samples // 2
     pair = 2
-    rows = bins // groups // CHUNKS * 2 * segs
+    rows = PART * 2 * segs
+    chunks = bins // groups // PART
     return pl.pallas_call(
         functools.partial(whiten_kernel, pair),
-        grid=(segs // pair,),
-        out_shape=jax.ShapeDtypeStruct((CHUNKS, groups, rows, block), jnp.bfloat16),
+        grid=(segs // (2 * pair),),
+        out_shape=jax.ShapeDtypeStruct((chunks, groups, rows, block), jnp.bfloat16),
         in_specs=[
-            pl.BlockSpec((pair, block, samples), lambda i: (i, 0, 0)),
+            pl.BlockSpec((2 * pair, block, samples), lambda i: (i, 0, 0)),
             pl.BlockSpec((2 * bins, samples), lambda i: (0, 0), pipeline_mode=pl.Buffered(1)),
         ],
-        out_specs=pl.BlockSpec((CHUNKS, groups, rows, block), lambda i: (0, 0, 0, 0)),
+        out_specs=pl.BlockSpec((chunks, groups, rows, block), lambda i: (0, 0, 0, 0)),
         scratch_shapes=[
-            pltpu.VMEM((bins + 16, pair * block), jnp.float32),
+            pltpu.VMEM((2, 2 * bins, pair * block), jnp.float32),
+            pltpu.VMEM((2, bins + 16, pair * block), jnp.float32),
             pltpu.VMEM((bins * 2 * segs, block), jnp.float32),
         ],
         compiler_params=pltpu.CompilerParams(vmem_limit_bytes=56 * MIB),
@@ -189,12 +206,12 @@
             device_id_type=pl.DeviceIdType.MESH,
         )
 
-    def shift(chunk):
+    def shift(chunk, slot):
         return pltpu.make_async_remote_copy(
-            src_ref=own.at[chunk],
-            dst_ref=following.at[chunk],
-            send_sem=shift_send.at[chunk],
-            recv_sem=shift_recv.at[chunk],
+            src_ref=own.at[chunk, slot],
+            dst_ref=following.at[chunk, slot],
+            send_sem=shift_send.at[chunk, slot],
+            recv_sem=shift_recv.at[chunk, slot],
             device_id={"chan": before},
             device_id_type=pl.DeviceIdType.MESH,
         )
@@ -236,13 +253,15 @@
         keep_white(chunk).start()
 
     def arrive(chunk):
-        for peer in peers:
+        keep_white(chunk).wait()
+        shift(chunk, me).start()
+        for peer in peers[::-1]:
             first(chunk, peer, peer).wait_recv()
-        keep_white(chunk).wait()
-        shift(chunk).start()
+            shift(chunk, peer).start()
 
     def work(chunk):
-        shift(chunk).wait_recv()
+        for slot in range(groups):
+            shift(chunk, slot).wait_recv()
         for which in range(SPANS):
 
             @pl.when(span == which)
@@ -257,26 +276,41 @@
             last(chunk, mate, mine).start()
         keep_stack(chunk).start()
 
-    start_first(0)
-    start_first(1)
+    for chunk in range(AHEAD):
+        start_first(chunk)
     down = lax.broadcasted_iota(jnp.int32, (block, 2 * rows), 0)
     across = lax.broadcasted_iota(jnp.int32, (block, 2 * rows), 1) % rows
     reverse = jnp.where(down + across == (span + 1) * rows - 1, 1.0, 0.0).astype(jnp.bfloat16)
-    for chunk in range(chunks):
+    arrive(0)
+
+    def steady(chunk, carry):
         arrive(chunk)
-        if chunk + 2 < chunks:
-            start_first(chunk + 2)
-        if chunk >= 1:
-            work(chunk - 1)
-    work(chunks - 1)
-    for chunk in range(chunks):
+        start_first(chunk + AHEAD)
+        work(chunk - 1)
+        return carry
+
+    def drain(chunk, carry):
+        arrive(chunk)
+        work(chunk - 1)
+        return carry
+
+    def finish(chunk, carry):
         for peer in peers:
             first(chunk, peer, peer).wait_send()
         for mate in mates:
             last(chunk, mate, mate).wait_send()
             last(chunk, mate, mate).wait_recv()
-        shift(chunk).wait_send()
+        for slot in range(groups):
+            shift(chunk, slot).wait_send()
         keep_stack(chunk).wait()
+        return carry
+
+    steady_end = chunks - AHEAD
+    start_first(AHEAD)
+    lax.fori_loop(1, steady_end, steady, 0)
+    lax.fori_loop(steady_end, chunks, drain, 0)
+    work(chunks - 1)
+    lax.fori_loop(0, chunks, finish, 0)
 
 
 def exchange(white, flags, ext_flags):
@@ -301,8 +335,8 @@
             pltpu.VMEM((2, width * (block // SPANS), block), jnp.float32),
             dma((chunks, groups)),
             dma((chunks, groups)),
-            dma((chunks,)),
-            dma((chunks,)),
+            dma((chunks, groups)),
+            dma((chunks, groups)),
             dma((chunks, members)),
             dma((chunks, members)),
             dma((2, chunks)),
@@ -324,10 +358,10 @@
     bins = samples // 2
     groups = lax.axis_size("tm")
     members = groups // SPANS
-    part = bins // members // CHUNKS
+    chunks = bins // members // PART
     table = jnp.asarray(forward_rows(samples, bins))
     inverse = inverse_rows(samples, bins, members, segs * groups)
-    inverse = inverse.reshape(members, 2, CHUNKS, part, samples)
+    inverse = inverse.reshape(members, 2, chunks, PART, samples)
     inverse = inverse.transpose(2, 0, 1, 3, 4).reshape(2 * bins, samples)
     flags = live.astype(jnp.bfloat16)
     next_flags = from_behind(flags, "chan", -1)
@@ -335,7 +369,7 @@
     rows = block // SPANS
     span = lax.axis_index("tm") // members
     span_flags = lax.dynamic_slice(flags.astype(jnp.float32), (span * rows,), (rows,))[::-1]
-    white = whiten(traces, table, members).reshape(CHUNKS, members, part, 2 * segs, block)
+    white = whiten(traces, table, members).reshape(chunks, members, PART, 2 * segs, block)
     stack = exchange(white, span_flags, ext_flags)
     lagged = lax.dot_general(
         stack.reshape(2 * bins, block // groups * block),

time: 302 us -> 297 us (0.983)
  Pallas kernels: 272 us -> 267 us
    pallas_call x1, Pallas kernels: 246 us -> 241 us  [exchange(): pl.pallas_call(functools.partial(exchange_kernel, lax.axis_size('chan')),...]
where the time goes in v4:
time: 297 us; the launch traced here: 294 us
  Pallas kernels  267 us (90%)
  matrix products  23.7 us (8%)
  starting transfers between devices  3.05 us (1%)
    pallas_call x1, Pallas kernels, exchange(): pl.pallas_call(functools.partial(exchange_kernel, lax.axis_size('chan')),...  241 us
    pallas_call x1, Pallas kernels, whiten(): pl.pallas_call(functools.partial(whiten_kernel, pair), grid=(segs // (2 *...  25.8 us
    dot_general x1, matrix products, body(): lax.dot_general(stack.reshape(2 * bins, block // groups * block), jnp.asa...  23.7 us
  transfers between devices with their start and end apart: 1, of which 0 were waited for; matrix products, arithmetic and copies ran while one was open for 0% of the time, Pallas kernels for 9%

profile of v4, /device:TPU:13, one launch (start us, length us, event | category | flops | bytes accessed | tf_op | source)
XLA Modules:
  0.0 294.2 jit_solution(464200918832619826)
XLA Ops:
  0.0 0.7 convert_bitcast_fusion
  0.7 3.0 %collective-permute-start = (bf16[128]{0:T(256)(128)(2,1)S(1)}, bf16[128]{0:T(256)(128)(2,1)S(1)}, u32[]{:S(2)}, u32[]{:S(2)}) collective-permute-start(bf16[128]{0:T(256)(128)(2,1)S(1)} %get-tuple-element.7), channel_id=1, source_target_pairs={{8,0},{16,8},{24,16},{9,1},{17,9},{25,17},{10,2},{18,10},{26,18},{... | collective-permute-start | bytes 776 | tf_op jit(solution)/shard_map/ppermute | solution.py:23
  3.7 25.8 %whiten.1 = bf16[16,4,256,128]{3,2,1,0:T(8,128)(2,1)} custom-call(bf16[8,128,2048]{2,1,0:T(8,128)(2,1)} %traces_ref.1, bf16[2048,2048]{1,0:T(8,128)(2,1)} %constant.29.clone.table_ref), custom_call_target="tpu_custom_call" | custom-call | flops 8589934592 | bytes 16777216 | tf_op jit(solution)/shard_map/whiten/pallas_call | solution.py:100
  29.6 0.1 dynamic_slice.3
  29.6 0.1 rev.3
  29.7 0.1 copy.5.flag_ref
  29.8 0.0 collective-permute-done
  29.8 240.7 %exchange.1 = bf16[16,4,2,16,2048]{4,3,2,1,0:T(8,128)(2,1)} custom-call(bf16[16,4,16,16,128]{4,3,2,1,0:T(8,128)(2,1)} %bitcast.12, f32[64,1]{1,0:T(8,128)S(1)} %copy.5.flag_ref, f32[1,256]{1,0:T(1,128)S(1)} %maximum_convert_fusion.ext_ref), custom_call_target="tpu_custom_call" | custom-call | flops 4294967296 | bytes 25165824 | tf_op jit(solution)/shard_map/exchange/pallas_call | solution.py:322
  270.5 23.7 %convolution_convert_fusion = bf16[2048,2048]{1,0:T(8,128)(2,1)} fusion(bf16[2048,2048]{1,0:T(8,128)(2,1)} %bitcast.11, bf16[2048,2048]{1,0:T(8,128)(2,1)} %constant.30.clone), kind=kOutput, calls=%fused_computation | convolution fusion | flops 17184063488 | bytes 25165824 | tf_op jit(solution)/shard_map/dot_general | solution.py:374
  (1 shorter events, 0.0 us)
Async XLA Ops:
  0.7 29.2 %collective-permute-start = (bf16[128]{0:T(256)(128)(2,1)S(1)}, bf16[128]{0:T(256)(128)(2,1)S(1)}, u32[]{:S(2)}, u32[]{:S(2)}) collective-permute-start(bf16[128]{0:T(256)(128)(2,1)S(1)} %get-tuple-element.7), channel_id=1, source_target_pairs={{8,0},{16,8},{24,16},{9,1},{17,9},{25,17},{10,2},{18,10},{26,18},{... | collective-permute-start | bytes 776 | tf_op jit(solution)/shard_map/ppermute | solution.py:23
